TPU v7x, 256 devices: a whole 4x4x8 slice. The times are simulated.
256 devices in a mesh: wave: 64 (over y, z, core), lev: 4 (over x).
Axes of the slice: x: 4, y: 4, z: 8, core: 2. Of those that a mesh axis runs over, the one named last changes fastest.
Arguments:
- spectral_even: bfloat16 [640, 641, 512], P('wave', None, 'lev'), may hold values from -0.125 to 0.125
- spectral_odd: bfloat16 [640, 640, 512], P('wave', None, 'lev'), may hold values from -0.125 to 0.125
- table_even: bfloat16 [640, 641, 128], P('wave'), may hold values from -0.15625 to 0.15625
- table_odd: bfloat16 [640, 640, 128], P('wave'), may hold values from -0.15625 to 0.15625
- slot_pair: int32 [640], replicated, may hold values from 0 to 639, each once
- slot_row: int32 [256], replicated, may hold values from 0 to 255, each once
- row_length: int32 [128], replicated, may hold values from 20 to 5136, as said below
Outputs:
- grid: bfloat16 [256, 256, 5632], P(('wave', 'lev'))
Inputs may be any that keep to these rules, and one draw needn't show every extreme that they name: `row_length`: each value is 4 j + 16 for a latitude index j from 1 to 1280, distinct over pairs; j = 1 and j = 1280 always occur.
All inputs are finite; a program needn't handle non-finite values.
Results may differ from a plain program's by a relative error of at most 0.0055.
Values may be sent and summed in bfloat16 or wider, within the bound.
A program may use at most 192 MiB of HBM per device.

v0:
```python
import math

import jax
import jax.numpy as jnp
from jax import lax
from jax.sharding import PartitionSpec as P

TRUNC = 1280
LPAD = 5632


block_width = 512


def split_terms(table, coeffs, count):
    position = jnp.arange(table.shape[1], dtype=jnp.int32)
    inside = (position[None, :] < count[:, None])[:, :, None]
    zeroes = jnp.zeros_like(table)
    first_table = jnp.where(inside, table, zeroes)
    second_table = jnp.where(inside, zeroes, table)
    first_sum = jnp.einsum("skp,skc->spc", first_table, coeffs, preferred_element_type=jnp.float32)
    second_sum = jnp.einsum(
        "skp,skc->spc", second_table, coeffs, preferred_element_type=jnp.float32
    )
    return jnp.stack([first_sum, second_sum], axis=1)


def direct_trig(product, length):
    phase = product.astype(jnp.float32) * (2.0 * math.pi) / length.astype(jnp.float32)
    return (jnp.cos(phase), jnp.sin(phase))


def grid_block(real_cols, imag_cols, wavenums, length, offset, make_trig):
    points = offset + jnp.arange(block_width, dtype=jnp.int32)
    product = wavenums[None, :] * points[:, None] % length
    cosine, sine = make_trig(product)
    active = 2 * wavenums < length
    factor = jnp.where(active, jnp.where(wavenums == 0, 1.0, 2.0), 0.0).astype(jnp.float32)
    real_basis = (factor[None, :] * cosine).astype(jnp.bfloat16)
    imag_basis = (-factor[None, :] * sine).astype(jnp.bfloat16)
    values = jnp.einsum("km,mv->vk", real_basis, real_cols, preferred_element_type=jnp.float32)
    values = values + jnp.einsum(
        "km,mv->vk", imag_basis, imag_cols, preferred_element_type=jnp.float32
    )
    return jnp.where(points[None, :] < length, values, 0.0).astype(jnp.bfloat16)


def shards(spectral_even, spectral_odd, table_even, table_odd, slot_pair, slot_row, row_length):
    slots_dev = spectral_even.shape[0]
    lev_count = lax.axis_size("lev")
    own_first = lax.dynamic_slice_in_dim(slot_pair, lax.axis_index("wave") * slots_dev, slots_dev)
    sym_part = split_terms(table_even, spectral_even, (TRUNC + 1 - own_first) // 2)
    anti_part = split_terms(table_odd, spectral_odd, (TRUNC - own_first) // 2)
    fourier = jnp.concatenate([sym_part + anti_part, sym_part - anti_part], axis=2).astype(
        jnp.bfloat16
    )
    ordered = jnp.take(fourier, slot_row, axis=2)
    partial_rows = lax.all_to_all(ordered, "wave", split_axis=2, concat_axis=0, tiled=True)
    own_rows = lax.all_to_all(partial_rows, "lev", split_axis=2, concat_axis=3, tiled=True)
    row_dev = own_rows.shape[2]
    levels = own_rows.shape[3] // 2
    pairs = row_length.shape[0]
    wavenums = jnp.stack([slot_pair, TRUNC - 1 - slot_pair], axis=1).reshape(-1)
    base_slot = (lax.axis_index("wave") * lev_count + lax.axis_index("lev")) * row_dev
    row_number = slot_row[base_slot + 0]
    length = row_length[row_number % pairs]
    columns = own_rows[:, :, 0, :].reshape(TRUNC, levels, 2)
    real_cols = columns[:, :, 0]
    imag_cols = columns[:, :, 1]

    def make_trig(product):
        return direct_trig(product, length)

    def add_block(number, current):
        offset = (number * block_width).astype(jnp.int32)
        piece = grid_block(real_cols, imag_cols, wavenums, length, offset, make_trig)
        return lax.dynamic_update_slice_in_dim(current, piece, offset, 1)

    empty_grid = jnp.zeros((levels, LPAD), jnp.bfloat16)
    results = [lax.fori_loop(0, LPAD // block_width, add_block, empty_grid)]
    return jnp.stack(results, axis=0)


def solution(mesh):
    in_specs = (
        P("wave", None, "lev"),
        P("wave", None, "lev"),
        P("wave", None, None),
        P("wave", None, None),
        P(),
        P(),
        P(),
    )
    out_specs = P(("wave", "lev"), None, None)
    return jax.shard_map(shards, mesh=mesh, in_specs=in_specs, out_specs=out_specs, check_vma=False)
```

profile of v0, /device:TPU:1, one launch (start us, length us, event | category | flops | bytes accessed | tf_op | source)
XLA Modules:
  0.0 1178.6 jit_solution(15124846935500131809)
XLA Ops:
  0.0 0.9 and_select_fusion.1
  1.5 4.6 fusion.34
  6.1 4.3 fusion.37
  10.6 3.8 fusion.40
  14.4 3.8 fusion.43
  18.7 1.4 copy.26
  20.1 5.4 gather_fusion
  25.5 2.6 fusion.33
  28.1 47.1 %all_to_all.27 = bf16[10,2,256,128]{3,1,0,2:T(2,128)(2,1)S(1)} all-to-all(bf16[10,2,256,128]{3,1,0,2:T(2,128)(2,1)S(1)} %fusion.33), channel_id=1, replica_groups=mesh['wave'=64,'lev'=4] {'wave'}, dimensions={2} | all-to-all | bytes 2621440 | tf_op jit(solution)/shard_map/all_to_all | solution.py:58
  75.9 2.1 copy.28
  78.0 4.3 all-to-all-start.1
  88.0 12.1 %all-to-all-done.1 = bf16[640,2,4,128]{3,1,0,2:T(2,128)(2,1)S(1)} async-done(((bf16[640,2,4,128]{3,1,0,2:T(2,128)(2,1)}), bf16[640,2,4,128]{3,1,0,2:T(2,128)(2,1)S(1)}, u32[]{:S(2)}, u32[]{:S(2)}) %all-to-all-start.1) | async-done | bytes 1310752 | tf_op jit(solution)/shard_map/all_to_all | solution.py:59
  100.1 2.7 copy.29
  102.9 182.6 %reshape_squeeze.3 = bf16[1280,256,2]{2,1,0:T(8,128)(2,1)} reshape(bf16[640,2,4,128]{3,2,1,0:T(4,128)(2,1)} %copy.29) | data formatting | bytes 2621440 | tf_op jit(solution)/shard_map/reshape;squeeze | solution.py:67
  285.5 83.6 %slice_reduce_fusion = (bf16[1280,256]{1,0:T(8,128)(2,1)S(1)}, bf16[1280,256]{1,0:T(8,128)(2,1)}) fusion(bf16[1280,256,2]{2,1,0:T(8,128)(2,1)} %reshape_squeeze.3), kind=kLoop, calls=%fused_computation.29 | loop fusion | bytes 2621440 | tf_op jit(solution)/shard_map/slice | solution.py:69
  369.1 1.8 broadcast_in_dim.108.clone
  370.9 806.6 %while.16 = (s32[]{:T(128)}, bf16[256,5632]{1,0:T(8,128)(2,1)}, s32[]{:T(128)}, s32[1280]{0:T(1024)S(1)}, s32[640,2]{1,0:T(8,128)}, /*index=5*/s32[]{:T(128)}, p...) while((s32[]{:T(128)}, bf16[256,5632]{1,0:T(8,128)(2,1)}, ...), condition=%wide.wide.region_1.2_spmd, body=%wide.wide.region_0.1_spmd.sunk | while | flops 688530432 | bytes 3713249 | solution.py:80
  371.7 35.3 %fusion.74 = f32[512,256]{1,0:T(8,128)S(1)} fusion(bf16[1280,256]{1,0:T(8,128)(2,1)S(1)} %get-tuple-element.390, f32[1280]{0:T(1024)S(1)} %get-tuple-element.350, f32[]{:T(128)} %get-tuple-element.389, s32[]{:T(128)} %get-tuple-element.387, s32[512]{0:T(512)S(1)} %iota_add_fusion.3, s32[1280]{0:T(1024)S(1)} %get-tuple-element.392, ...), kind=kOutput, calls=%fused_computation.12.clone.clone.1 | convolution fusion | flops 344064000 | bytes 1191945 | tf_op jit(solution)/shard_map/while/body/eval_jaxpr/km,mv->vk/dot_general | solution.py:41
  407.7 35.5 %fusion.75 = bf16[256,512]{0,1:T(8,128)(2,1)S(1)} fusion(f32[512,256]{1,0:T(8,128)S(1)} %fusion.74, bf16[1280,256]{1,0:T(8,128)(2,1)S(1)} %get-tuple-element.391, f32[1280]{0:T(1024)S(1)} %get-tuple-element.351, f32[]{:T(128)} %get-tuple-element.389, pred[]{:T(512)} %get-tuple-element.388, s32[]{:T(128)} %get-tuple-element.387, ...), kind=kOutput, calls=%fused_computation.19.clone.clone.1 | convolution fusion | flops 344457216 | bytes 1454601 | tf_op jit(solution)/shard_map/while/body/eval_jaxpr/km,mv->vk/dot_general | solution.py:42
  443.3 0.7 constant_dynamic-update-slice_fusion.3
  445.1 35.3 %fusion.74 = f32[512,256]{1,0:T(8,128)S(1)} fusion(bf16[1280,256]{1,0:T(8,128)(2,1)S(1)} %get-tuple-element.390, f32[1280]{0:T(1024)S(1)} %get-tuple-element.350, f32[]{:T(128)} %get-tuple-element.389, s32[]{:T(128)} %get-tuple-element.387, s32[512]{0:T(512)S(1)} %iota_add_fusion.3, s32[1280]{0:T(1024)S(1)} %get-tuple-element.392, ...), kind=kOutput, calls=%fused_computation.12.clone.clone.1 | convolution fusion | flops 344064000 | bytes 1191945 | tf_op jit(solution)/shard_map/while/body/eval_jaxpr/km,mv->vk/dot_general | solution.py:41
  481.1 35.5 %fusion.75 = bf16[256,512]{0,1:T(8,128)(2,1)S(1)} fusion(f32[512,256]{1,0:T(8,128)S(1)} %fusion.74, bf16[1280,256]{1,0:T(8,128)(2,1)S(1)} %get-tuple-element.391, f32[1280]{0:T(1024)S(1)} %get-tuple-element.351, f32[]{:T(128)} %get-tuple-element.389, pred[]{:T(512)} %get-tuple-element.388, s32[]{:T(128)} %get-tuple-element.387, ...), kind=kOutput, calls=%fused_computation.19.clone.clone.1 | convolution fusion | flops 344457216 | bytes 1454601 | tf_op jit(solution)/shard_map/while/body/eval_jaxpr/km,mv->vk/dot_general | solution.py:42
  516.7 0.7 constant_dynamic-update-slice_fusion.3
  518.3 35.3 %fusion.74 = f32[512,256]{1,0:T(8,128)S(1)} fusion(bf16[1280,256]{1,0:T(8,128)(2,1)S(1)} %get-tuple-element.390, f32[1280]{0:T(1024)S(1)} %get-tuple-element.350, f32[]{:T(128)} %get-tuple-element.389, s32[]{:T(128)} %get-tuple-element.387, s32[512]{0:T(512)S(1)} %iota_add_fusion.3, s32[1280]{0:T(1024)S(1)} %get-tuple-element.392, ...), kind=kOutput, calls=%fused_computation.12.clone.clone.1 | convolution fusion | flops 344064000 | bytes 1191945 | tf_op jit(solution)/shard_map/while/body/eval_jaxpr/km,mv->vk/dot_general | solution.py:41
  554.2 35.5 %fusion.75 = bf16[256,512]{0,1:T(8,128)(2,1)S(1)} fusion(f32[512,256]{1,0:T(8,128)S(1)} %fusion.74, bf16[1280,256]{1,0:T(8,128)(2,1)S(1)} %get-tuple-element.391, f32[1280]{0:T(1024)S(1)} %get-tuple-element.351, f32[]{:T(128)} %get-tuple-element.389, pred[]{:T(512)} %get-tuple-element.388, s32[]{:T(128)} %get-tuple-element.387, ...), kind=kOutput, calls=%fused_computation.19.clone.clone.1 | convolution fusion | flops 344457216 | bytes 1454601 | tf_op jit(solution)/shard_map/while/body/eval_jaxpr/km,mv->vk/dot_general | solution.py:42
  589.9 0.7 constant_dynamic-update-slice_fusion.3
  591.5 35.3 %fusion.74 = f32[512,256]{1,0:T(8,128)S(1)} fusion(bf16[1280,256]{1,0:T(8,128)(2,1)S(1)} %get-tuple-element.390, f32[1280]{0:T(1024)S(1)} %get-tuple-element.350, f32[]{:T(128)} %get-tuple-element.389, s32[]{:T(128)} %get-tuple-element.387, s32[512]{0:T(512)S(1)} %iota_add_fusion.3, s32[1280]{0:T(1024)S(1)} %get-tuple-element.392, ...), kind=kOutput, calls=%fused_computation.12.clone.clone.1 | convolution fusion | flops 344064000 | bytes 1191945 | tf_op jit(solution)/shard_map/while/body/eval_jaxpr/km,mv->vk/dot_general | solution.py:41
  627.4 35.5 %fusion.75 = bf16[256,512]{0,1:T(8,128)(2,1)S(1)} fusion(f32[512,256]{1,0:T(8,128)S(1)} %fusion.74, bf16[1280,256]{1,0:T(8,128)(2,1)S(1)} %get-tuple-element.391, f32[1280]{0:T(1024)S(1)} %get-tuple-element.351, f32[]{:T(128)} %get-tuple-element.389, pred[]{:T(512)} %get-tuple-element.388, s32[]{:T(128)} %get-tuple-element.387, ...), kind=kOutput, calls=%fused_computation.19.clone.clone.1 | convolution fusion | flops 344457216 | bytes 1454601 | tf_op jit(solution)/shard_map/while/body/eval_jaxpr/km,mv->vk/dot_general | solution.py:42
  663.1 0.7 constant_dynamic-update-slice_fusion.3
  664.9 35.3 %fusion.74 = f32[512,256]{1,0:T(8,128)S(1)} fusion(bf16[1280,256]{1,0:T(8,128)(2,1)S(1)} %get-tuple-element.390, f32[1280]{0:T(1024)S(1)} %get-tuple-element.350, f32[]{:T(128)} %get-tuple-element.389, s32[]{:T(128)} %get-tuple-element.387, s32[512]{0:T(512)S(1)} %iota_add_fusion.3, s32[1280]{0:T(1024)S(1)} %get-tuple-element.392, ...), kind=kOutput, calls=%fused_computation.12.clone.clone.1 | convolution fusion | flops 344064000 | bytes 1191945 | tf_op jit(solution)/shard_map/while/body/eval_jaxpr/km,mv->vk/dot_general | solution.py:41
  700.8 35.5 %fusion.75 = bf16[256,512]{0,1:T(8,128)(2,1)S(1)} fusion(f32[512,256]{1,0:T(8,128)S(1)} %fusion.74, bf16[1280,256]{1,0:T(8,128)(2,1)S(1)} %get-tuple-element.391, f32[1280]{0:T(1024)S(1)} %get-tuple-element.351, f32[]{:T(128)} %get-tuple-element.389, pred[]{:T(512)} %get-tuple-element.388, s32[]{:T(128)} %get-tuple-element.387, ...), kind=kOutput, calls=%fused_computation.19.clone.clone.1 | convolution fusion | flops 344457216 | bytes 1454601 | tf_op jit(solution)/shard_map/while/body/eval_jaxpr/km,mv->vk/dot_general | solution.py:42
  736.5 0.7 constant_dynamic-update-slice_fusion.3
  738.0 35.3 %fusion.74 = f32[512,256]{1,0:T(8,128)S(1)} fusion(bf16[1280,256]{1,0:T(8,128)(2,1)S(1)} %get-tuple-element.390, f32[1280]{0:T(1024)S(1)} %get-tuple-element.350, f32[]{:T(128)} %get-tuple-element.389, s32[]{:T(128)} %get-tuple-element.387, s32[512]{0:T(512)S(1)} %iota_add_fusion.3, s32[1280]{0:T(1024)S(1)} %get-tuple-element.392, ...), kind=kOutput, calls=%fused_computation.12.clone.clone.1 | convolution fusion | flops 344064000 | bytes 1191945 | tf_op jit(solution)/shard_map/while/body/eval_jaxpr/km,mv->vk/dot_general | solution.py:41
  774.0 35.5 %fusion.75 = bf16[256,512]{0,1:T(8,128)(2,1)S(1)} fusion(f32[512,256]{1,0:T(8,128)S(1)} %fusion.74, bf16[1280,256]{1,0:T(8,128)(2,1)S(1)} %get-tuple-element.391, f32[1280]{0:T(1024)S(1)} %get-tuple-element.351, f32[]{:T(128)} %get-tuple-element.389, pred[]{:T(512)} %get-tuple-element.388, s32[]{:T(128)} %get-tuple-element.387, ...), kind=kOutput, calls=%fused_computation.19.clone.clone.1 | convolution fusion | flops 344457216 | bytes 1454601 | tf_op jit(solution)/shard_map/while/body/eval_jaxpr/km,mv->vk/dot_general | solution.py:42
  809.6 0.7 constant_dynamic-update-slice_fusion.3
  811.2 35.3 %fusion.74 = f32[512,256]{1,0:T(8,128)S(1)} fusion(bf16[1280,256]{1,0:T(8,128)(2,1)S(1)} %get-tuple-element.390, f32[1280]{0:T(1024)S(1)} %get-tuple-element.350, f32[]{:T(128)} %get-tuple-element.389, s32[]{:T(128)} %get-tuple-element.387, s32[512]{0:T(512)S(1)} %iota_add_fusion.3, s32[1280]{0:T(1024)S(1)} %get-tuple-element.392, ...), kind=kOutput, calls=%fused_computation.12.clone.clone.1 | convolution fusion | flops 344064000 | bytes 1191945 | tf_op jit(solution)/shard_map/while/body/eval_jaxpr/km,mv->vk/dot_general | solution.py:41
  847.2 35.5 %fusion.75 = bf16[256,512]{0,1:T(8,128)(2,1)S(1)} fusion(f32[512,256]{1,0:T(8,128)S(1)} %fusion.74, bf16[1280,256]{1,0:T(8,128)(2,1)S(1)} %get-tuple-element.391, f32[1280]{0:T(1024)S(1)} %get-tuple-element.351, f32[]{:T(128)} %get-tuple-element.389, pred[]{:T(512)} %get-tuple-element.388, s32[]{:T(128)} %get-tuple-element.387, ...), kind=kOutput, calls=%fused_computation.19.clone.clone.1 | convolution fusion | flops 344457216 | bytes 1454601 | tf_op jit(solution)/shard_map/while/body/eval_jaxpr/km,mv->vk/dot_general | solution.py:42
  884.6 35.3 %fusion.74 = f32[512,256]{1,0:T(8,128)S(1)} fusion(bf16[1280,256]{1,0:T(8,128)(2,1)S(1)} %get-tuple-element.390, f32[1280]{0:T(1024)S(1)} %get-tuple-element.350, f32[]{:T(128)} %get-tuple-element.389, s32[]{:T(128)} %get-tuple-element.387, s32[512]{0:T(512)S(1)} %iota_add_fusion.3, s32[1280]{0:T(1024)S(1)} %get-tuple-element.392, ...), kind=kOutput, calls=%fused_computation.12.clone.clone.1 | convolution fusion | flops 344064000 | bytes 1191945 | tf_op jit(solution)/shard_map/while/body/eval_jaxpr/km,mv->vk/dot_general | solution.py:41
  920.6 35.5 %fusion.75 = bf16[256,512]{0,1:T(8,128)(2,1)S(1)} fusion(f32[512,256]{1,0:T(8,128)S(1)} %fusion.74, bf16[1280,256]{1,0:T(8,128)(2,1)S(1)} %get-tuple-element.391, f32[1280]{0:T(1024)S(1)} %get-tuple-element.351, f32[]{:T(128)} %get-tuple-element.389, pred[]{:T(512)} %get-tuple-element.388, s32[]{:T(128)} %get-tuple-element.387, ...), kind=kOutput, calls=%fused_computation.19.clone.clone.1 | convolution fusion | flops 344457216 | bytes 1454601 | tf_op jit(solution)/shard_map/while/body/eval_jaxpr/km,mv->vk/dot_general | solution.py:42
  957.8 35.3 %fusion.74 = f32[512,256]{1,0:T(8,128)S(1)} fusion(bf16[1280,256]{1,0:T(8,128)(2,1)S(1)} %get-tuple-element.390, f32[1280]{0:T(1024)S(1)} %get-tuple-element.350, f32[]{:T(128)} %get-tuple-element.389, s32[]{:T(128)} %get-tuple-element.387, s32[512]{0:T(512)S(1)} %iota_add_fusion.3, s32[1280]{0:T(1024)S(1)} %get-tuple-element.392, ...), kind=kOutput, calls=%fused_computation.12.clone.clone.1 | convolution fusion | flops 344064000 | bytes 1191945 | tf_op jit(solution)/shard_map/while/body/eval_jaxpr/km,mv->vk/dot_general | solution.py:41
  993.7 35.5 %fusion.75 = bf16[256,512]{0,1:T(8,128)(2,1)S(1)} fusion(f32[512,256]{1,0:T(8,128)S(1)} %fusion.74, bf16[1280,256]{1,0:T(8,128)(2,1)S(1)} %get-tuple-element.391, f32[1280]{0:T(1024)S(1)} %get-tuple-element.351, f32[]{:T(128)} %get-tuple-element.389, pred[]{:T(512)} %get-tuple-element.388, s32[]{:T(128)} %get-tuple-element.387, ...), kind=kOutput, calls=%fused_computation.19.clone.clone.1 | convolution fusion | flops 344457216 | bytes 1454601 | tf_op jit(solution)/shard_map/while/body/eval_jaxpr/km,mv->vk/dot_general | solution.py:42
  1029.4 0.7 constant_dynamic-update-slice_fusion.3
  1031.0 35.3 %fusion.74 = f32[512,256]{1,0:T(8,128)S(1)} fusion(bf16[1280,256]{1,0:T(8,128)(2,1)S(1)} %get-tuple-element.390, f32[1280]{0:T(1024)S(1)} %get-tuple-element.350, f32[]{:T(128)} %get-tuple-element.389, s32[]{:T(128)} %get-tuple-element.387, s32[512]{0:T(512)S(1)} %iota_add_fusion.3, s32[1280]{0:T(1024)S(1)} %get-tuple-element.392, ...), kind=kOutput, calls=%fused_computation.12.clone.clone.1 | convolution fusion | flops 344064000 | bytes 1191945 | tf_op jit(solution)/shard_map/while/body/eval_jaxpr/km,mv->vk/dot_general | solution.py:41
  1066.9 35.5 %fusion.75 = bf16[256,512]{0,1:T(8,128)(2,1)S(1)} fusion(f32[512,256]{1,0:T(8,128)S(1)} %fusion.74, bf16[1280,256]{1,0:T(8,128)(2,1)S(1)} %get-tuple-element.391, f32[1280]{0:T(1024)S(1)} %get-tuple-element.351, f32[]{:T(128)} %get-tuple-element.389, pred[]{:T(512)} %get-tuple-element.388, s32[]{:T(128)} %get-tuple-element.387, ...), kind=kOutput, calls=%fused_computation.19.clone.clone.1 | convolution fusion | flops 344457216 | bytes 1454601 | tf_op jit(solution)/shard_map/while/body/eval_jaxpr/km,mv->vk/dot_general | solution.py:42
  1102.6 0.7 constant_dynamic-update-slice_fusion.3
  1104.4 35.3 %fusion.74 = f32[512,256]{1,0:T(8,128)S(1)} fusion(bf16[1280,256]{1,0:T(8,128)(2,1)S(1)} %get-tuple-element.390, f32[1280]{0:T(1024)S(1)} %get-tuple-element.350, f32[]{:T(128)} %get-tuple-element.389, s32[]{:T(128)} %get-tuple-element.387, s32[512]{0:T(512)S(1)} %iota_add_fusion.3, s32[1280]{0:T(1024)S(1)} %get-tuple-element.392, ...), kind=kOutput, calls=%fused_computation.12.clone.clone.1 | convolution fusion | flops 344064000 | bytes 1191945 | tf_op jit(solution)/shard_map/while/body/eval_jaxpr/km,mv->vk/dot_general | solution.py:41
  1140.3 35.5 %fusion.75 = bf16[256,512]{0,1:T(8,128)(2,1)S(1)} fusion(f32[512,256]{1,0:T(8,128)S(1)} %fusion.74, bf16[1280,256]{1,0:T(8,128)(2,1)S(1)} %get-tuple-element.391, f32[1280]{0:T(1024)S(1)} %get-tuple-element.351, f32[]{:T(128)} %get-tuple-element.389, pred[]{:T(512)} %get-tuple-element.388, s32[]{:T(128)} %get-tuple-element.387, ...), kind=kOutput, calls=%fused_computation.19.clone.clone.1 | convolution fusion | flops 344457216 | bytes 1454601 | tf_op jit(solution)/shard_map/while/body/eval_jaxpr/km,mv->vk/dot_general | solution.py:42
  1176.0 0.7 constant_dynamic-update-slice_fusion.3
  (81 shorter events, 20.5 us)
Async XLA Ops:
  0.0 1.5 copy-start
  1.5 4.7 copy-start.5
  6.1 4.4 copy-start.6
  6.1 4.4 copy-start.7
  14.4 3.8 copy-start.4
  78.0 6.9 copy-start.8
  78.0 8.7 copy-start.3
  78.0 22.2 %all-to-all-start.1 = ((bf16[640,2,4,128]{3,1,0,2:T(2,128)(2,1)}), bf16[640,2,4,128]{3,1,0,2:T(2,128)(2,1)S(1)}, u32[]{:S(2)}, u32[]{:S(2)}) async-start(bf16[640,2,4,128]{3,1,0,2:T(2,128)(2,1)} %copy.28), calls=%async_computation.1 | async-start | bytes 2621440 | tf_op jit(solution)/shard_map/all_to_all | solution.py:59
  87.0 198.5 %copy-start.1 = (s32[640,2]{1,0:T(8,128)}, s32[640,2]{1,0:T(8,128)S(1)}, u32[]{:S(2)}) copy-start(s32[640,2]{1,0:T(8,128)S(1)} %copy.23) | copy-start | bytes 15364
  369.1 1.8 copy-start.2
where the time goes:
time: 1190 us; the launch traced here: 1180 us
  matrix products  796 us (67%)
  local copies, waits for them, and re-layouts  292 us (25%)
  blocking collectives  47.1 us (4%)
  other arithmetic  18 us (2%)
  waiting for transfers between devices  12.1 us (1%)
    dot_general x11, matrix products, grid_block(): jnp.einsum('km,mv->vk', imag_basis, imag_cols, preferred_element_type=jnp...  390 us
    dot_general x11, matrix products, grid_block(): jnp.einsum('km,mv->vk', real_basis, real_cols, preferred_element_type=jnp...  389 us
    another operation x1, local copies, waits for them, and re-layouts, shards(): columns = own_rows[:, :, 0, :].reshape(TRUNC, levels, 2)  183 us
    slice x1, local copies, waits for them, and re-layouts, shards(): imag_cols = columns[:, :, 1]  83.6 us
    all_to_all x1, blocking collectives, shards(): lax.all_to_all(ordered, 'wave', split_axis=2, concat_axis=0, tiled=True)  47.1 us
  transfers between devices with their start and end apart: 1, of which 1 were waited for; matrix products, arithmetic and copies ran while one was open for 0% of the time, Pallas kernels for 0%

commit v1 on v0

v1 whole, which is shorter than its diff:
```python
import math

import jax
import jax.numpy as jnp
from jax import lax
from jax.experimental import pallas as pl
from jax.experimental.pallas import tpu as pltpu
from jax.sharding import PartitionSpec as P

TRUNC = 1280
SLOTS = 640
LPAD = 5632
ROWS = 256
PAIRS = 128
WAVE = 64
LEV = 4
SLOTS_DEV = 10
MESSAGE = 2 * SLOTS_DEV
STEP_SLOTS = 2
STEPS = SLOTS_DEV // STEP_SLOTS
QUARTER_PAD = 1536
LANES = 128
BLOCK = 256
BLOCKS = QUARTER_PAD // BLOCK
CHUNK = 8

MESH = pl.DeviceIdType.MESH
VMEM = pltpu.VMEM
SMEM = pltpu.SMEM
F32 = jnp.float32
BF16 = jnp.bfloat16
TN = (((0,), (0,)), ((), ()))
NT = (((1,), (1,)), ((), ()))


def lane_iota(rows):
    return lax.broadcasted_iota(jnp.int32, (rows, LANES), 1)


def unit_circle(product, length, inverse):
    rest = product - jnp.floor(product * inverse) * length
    quarters = rest * (4.0 * inverse)
    nearest = jnp.floor(quarters + 0.5)
    angle = (quarters - nearest) * (0.5 * math.pi)
    z = angle * angle
    sine = angle * (1.0 + z * (-1.0 / 6 + z * (1.0 / 120 + z * (-1.0 / 5040 + z * (1.0 / 362880)))))
    cosine = 1.0 + z * (-0.5 + z * (1.0 / 24 + z * (-1.0 / 720 + z * (1.0 / 40320))))
    quadrant = nearest.astype(jnp.int32)
    odd = (quadrant & 1) == 1
    cos_out = jnp.where(odd, sine, cosine)
    sin_out = jnp.where(odd, cosine, sine)
    cos_out = jnp.where(((quadrant + 1) & 2) == 2, -cos_out, cos_out)
    sin_out = jnp.where((quadrant & 2) == 2, -sin_out, sin_out)
    return cos_out, sin_out


def masked_halves(coeffs, count, flip):
    rows = coeffs.shape[0]
    position = lax.broadcasted_iota(jnp.int32, (rows, LANES), 0)
    first = jnp.where(position < count, 1.0, 0.0)
    chosen = (flip + (1.0 - 2.0 * flip) * first).astype(BF16)
    even = coeffs * chosen
    return jnp.concatenate([even, coeffs - even], axis=1)


def exchange_kernel(
    pair_s,
    row_s,
    length_s,
    pair_v,
    row_v,
    spec_even,
    spec_odd,
    tab_even,
    tab_odd,
    recv,
    basis_out,
    permute,
    spread,
    send,
    waves,
    basis,
    send_sem,
    recv_sem,
    self_sem,
    basis_sem,
    line_sem,
):
    step = pl.program_id(0)
    w = lax.axis_index("wave")
    l = lax.axis_index("lev")
    me = w * LEV + l
    my_slot = l * WAVE + w
    barrier = pltpu.get_barrier_semaphore()

    @pl.when(step == 0)
    def _():
        def greet(i, carry):
            pl.semaphore_signal(
                barrier, inc=1, device_id=(lax.rem(w + i, WAVE), l), device_id_type=MESH
            )
            return carry

        lax.fori_loop(1, WAVE, greet, 0)
        for i in range(1, LEV):
            pl.semaphore_signal(
                barrier, inc=1, device_id=(w, lax.rem(l + i, LEV)), device_id_type=MESH
            )
        source = lax.broadcasted_iota(jnp.int32, (ROWS, ROWS), 0)
        hot = jnp.where(source == row_v[...], 1.0, 0.0)
        permute[...] = hot.T.astype(BF16)

    @pl.when(step == STEPS - 2)
    def _():
        pl.semaphore_wait(barrier, WAVE - 1 + LEV - 1)
        for i in range(1, LEV):
            pl.semaphore_signal(
                line_sem, inc=1, device_id=(w, lax.rem(l + i, LEV)), device_id_type=MESH
            )

    for j in range(STEP_SLOTS):
        slot = step * STEP_SLOTS + j
        first = pair_s[w * SLOTS_DEV + slot]
        flip = (first & 1).astype(F32)
        even_terms = masked_halves(spec_even[j], (TRUNC + 1 - first) >> 1, flip)
        odd_terms = masked_halves(spec_odd[j], (TRUNC - first) >> 1, flip)
        sym = lax.dot_general(tab_even[j], even_terms, TN, preferred_element_type=F32)
        anti = lax.dot_general(tab_odd[j], odd_terms, TN, preferred_element_type=F32)
        rows = jnp.concatenate([sym + anti, sym - anti], axis=0).astype(BF16)
        ordered = jnp.dot(permute[...], rows, preferred_element_type=F32)
        spread[pl.ds(slot, ROWS, stride=MESSAGE), :] = ordered[:, :LANES]
        spread[pl.ds(slot + SLOTS_DEV, ROWS, stride=MESSAGE), :] = ordered[:, LANES:]

    @pl.when(step == STEPS - 1)
    def _():
        pl.semaphore_wait(line_sem, LEV - 1)

        def send_chunk(i, carry):
            chunk = lax.rem(me // CHUNK + i, ROWS // CHUNK)
            start = pl.multiple_of(chunk * CHUNK * MESSAGE, CHUNK * MESSAGE)
            block = spread[pl.ds(start, CHUNK * MESSAGE), :].astype(BF16)
            send[pl.ds(chunk * CHUNK, CHUNK)] = block.reshape(CHUNK, MESSAGE // 2, 2, LANES)
            for j in range(CHUNK):
                target = chunk * CHUNK + lax.rem(me + j, CHUNK)

                @pl.when(target != me)
                def _():
                    pltpu.make_async_remote_copy(
                        src_ref=send.at[target],
                        dst_ref=recv.at[my_slot],
                        send_sem=send_sem,
                        recv_sem=recv_sem,
                        device_id=(target // LEV, lax.rem(target, LEV)),
                        device_id_type=MESH,
                    ).start()

            return carry

        lax.fori_loop(0, ROWS // CHUNK, send_chunk, 0)
        own = pltpu.make_async_copy(send.at[me], recv.at[my_slot], self_sem)
        own.start()

        length = length_s[row_s[me] & (PAIRS - 1)].astype(F32)
        inverse = 1.0 / jnp.full((16, LANES), length, F32)
        for i in range(SLOTS // LANES):
            pair = pair_v[:, i * LANES : (i + 1) * LANES]
            even = jnp.where((pair & 1) == 0, pair, TRUNC - 1 - pair).astype(F32)
            waves[i * LANES : (i + 1) * LANES, :] = jnp.broadcast_to(even, (LANES, LANES)).T

        lane = lane_iota(16).astype(F32)

        def basis_rows(i, carry):
            at = pl.multiple_of(i * 16, 16)
            even = waves[pl.ds(at, 16), :]
            for parity in range(2):
                number = even if parity == 0 else (TRUNC - 1.0) - even
                factor = jnp.where(
                    2.0 * number < length, jnp.where(number == 0.0, 1.0, 2.0), 0.0
                )
                cosine, sine = unit_circle(number * lane, length, inverse)
                turn_cos, turn_sin = unit_circle(number * float(LANES), length, inverse)
                real = factor * cosine
                imag = -factor * sine
                for k in range(QUARTER_PAD // LANES):
                    columns = slice(k * LANES, (k + 1) * LANES)
                    basis[parity, pl.ds(at, 16), columns] = real.astype(BF16)
                    low = pl.multiple_of(at + SLOTS, 16)
                    basis[parity, pl.ds(low, 16), columns] = imag.astype(BF16)
                    real, imag = (
                        real * turn_cos + imag * turn_sin,
                        imag * turn_cos - real * turn_sin,
                    )
            return carry

        lax.fori_loop(0, SLOTS // 16, basis_rows, 0)
        out = pltpu.make_async_copy(basis, basis_out, basis_sem)
        out.start()

        own.wait()
        others = pl.ds(0, ROWS - 1)
        pltpu.make_async_copy(send.at[others], recv.at[others], recv_sem).wait()
        pltpu.make_async_copy(send.at[others], recv.at[others], send_sem).wait()
        out.wait()


def fourier_kernel(row_s, length_s, pair_v, recv, basis, grid_out, left, total):
    step = pl.program_id(0)
    me = lax.axis_index("wave") * LEV + lax.axis_index("lev")
    quarter = length_s[row_s[me] & (PAIRS - 1)] >> 2

    @pl.when(step == 0)
    def _():
        total[...] = jnp.zeros_like(total)
        row = lax.broadcasted_iota(jnp.int32, (LANES, LANES), 0)
        column = lane_iota(LANES)
        wanted = jnp.where(row < 64, 2 * row, 2 * row - 127)
        pick = jnp.where(column == wanted, 1.0, 0.0).astype(BF16)
        pair = pair_v[...]
        for parity in range(2):
            number = jnp.where((pair & 1) == parity, pair, TRUNC - 1 - pair)
            second = ((number >> 1) & 1).astype(F32)
            sign = 1.0 - 2.0 * second if parity == 0 else 2.0 * second - 1.0
            for l in range(LEV):
                block = recv[l * WAVE : (l + 1) * WAVE, parity * 5 : parity * 5 + 5]
                block = block.reshape(SLOTS, LANES)
                parts = lax.dot_general(pick, block, NT, preferred_element_type=F32)
                real, imag = parts[:64], parts[64:]
                top = slice(l * 64, l * 64 + 64)
                low = slice(256 + l * 64, 256 + l * 64 + 64)
                left[parity, top, :SLOTS] = real.astype(BF16)
                left[parity, top, SLOTS:] = imag.astype(BF16)
                if parity == 0:
                    left[parity, low, :SLOTS] = (real * sign).astype(BF16)
                    left[parity, low, SLOTS:] = (imag * sign).astype(BF16)
                else:
                    left[parity, low, :SLOTS] = (imag * sign).astype(BF16)
                    left[parity, low, SLOTS:] = (real * -sign).astype(BF16)

    even = jnp.dot(left[0], basis[0], preferred_element_type=F32)
    odd = jnp.dot(left[1], basis[1], preferred_element_type=F32)
    point = step * BLOCK + lax.broadcasted_iota(jnp.int32, (256, BLOCK), 1)
    inside = point < quarter
    lane = lane_iota(256)
    for c in range(4):
        half = slice((c & 1) * 256, (c & 1) * 256 + 256)
        value = even[half] + odd[half] if c < 2 else even[half] - odd[half]
        value = jnp.where(inside, value, 0.0)
        offset = c * quarter + step * BLOCK
        shift = offset & (LANES - 1)
        start = pl.multiple_of(offset - shift, LANES)
        turned = [pltpu.roll(value[:, :LANES], shift, 1), pltpu.roll(value[:, LANES:], shift, 1)]
        before = lane < shift
        zero = jnp.zeros_like(turned[0])
        pieces = [
            jnp.where(before, zero, turned[0]),
            jnp.where(before, turned[0], turned[1]),
            jnp.where(before, turned[1], zero),
        ]
        for i, piece in enumerate(pieces):
            where = pl.ds(pl.multiple_of(start + i * LANES, LANES), LANES)
            total[:, where] += piece

    @pl.when(step == BLOCKS - 1)
    def _():
        grid_out[0] = total[:, :LPAD].astype(BF16)


def shards(spectral_even, spectral_odd, table_even, table_odd, slot_pair, slot_row, row_length):
    pair_row = slot_pair.reshape(1, SLOTS)
    order_row = slot_row.reshape(1, ROWS)
    in_smem = pl.BlockSpec(memory_space=SMEM)
    in_vmem = pl.BlockSpec(memory_space=VMEM)
    anywhere = pl.BlockSpec(memory_space=pl.ANY)

    def by_slot(array):
        return pl.BlockSpec((STEP_SLOTS,) + array.shape[1:], lambda i: (i, 0, 0))

    message = (MESSAGE // 2, 2, LANES)
    recv, basis = pl.pallas_call(
        exchange_kernel,
        grid=(STEPS,),
        out_shape=[
            jax.ShapeDtypeStruct((ROWS,) + message, BF16),
            jax.ShapeDtypeStruct((2, TRUNC, QUARTER_PAD), BF16),
        ],
        in_specs=[in_smem] * 3
        + [in_vmem] * 2
        + [by_slot(a) for a in (spectral_even, spectral_odd, table_even, table_odd)],
        out_specs=[anywhere, anywhere],
        scratch_shapes=[
            VMEM((ROWS, ROWS), BF16),
            VMEM((ROWS * MESSAGE, LANES), F32),
            VMEM((ROWS,) + message, BF16),
            VMEM((SLOTS, LANES), F32),
            VMEM((2, TRUNC, QUARTER_PAD), BF16),
            pltpu.SemaphoreType.DMA,
            pltpu.SemaphoreType.DMA,
            pltpu.SemaphoreType.DMA,
            pltpu.SemaphoreType.DMA,
            pltpu.SemaphoreType.REGULAR,
        ],
        name="legendre_exchange",
        compiler_params=pltpu.CompilerParams(
            collective_id=0, has_side_effects=True, vmem_limit_bytes=40 << 20
        ),
        cost_estimate=pl.CostEstimate(
            flops=2 * SLOTS_DEV * 1281 * 128 * 256, bytes_accessed=16 << 20, transcendentals=0
        ),
    )(
        slot_pair,
        slot_row,
        row_length,
        pair_row,
        order_row,
        spectral_even,
        spectral_odd,
        table_even,
        table_odd,
    )
    return pl.pallas_call(
        fourier_kernel,
        grid=(BLOCKS,),
        out_shape=jax.ShapeDtypeStruct((1, 256, LPAD), BF16),
        in_specs=[
            in_smem,
            in_smem,
            in_vmem,
            in_vmem,
            pl.BlockSpec((2, TRUNC, BLOCK), lambda i: (0, 0, i)),
        ],
        out_specs=pl.BlockSpec((1, 256, LPAD), lambda i: (0, 0, 0)),
        scratch_shapes=[
            VMEM((2, 512, TRUNC), BF16),
            VMEM((256, LPAD + 2 * LANES), F32),
        ],
        name="fourier",
        compiler_params=pltpu.CompilerParams(vmem_limit_bytes=40 << 20),
        cost_estimate=pl.CostEstimate(
            flops=4 * 512 * TRUNC * QUARTER_PAD, bytes_accessed=12 << 20, transcendentals=0
        ),
    )(slot_row, row_length, pair_row, recv, basis)


def solution(mesh):
    in_specs = (
        P("wave", None, "lev"),
        P("wave", None, "lev"),
        P("wave", None, None),
        P("wave", None, None),
        P(),
        P(),
        P(),
    )
    out_specs = P(("wave", "lev"), None, None)
    return jax.shard_map(shards, mesh=mesh, in_specs=in_specs, out_specs=out_specs, check_vma=False)
```

time: 1190 us -> 69.8 us (0.06)
  matrix products: 796 us -> 0 us
  local copies, waits for them, and re-layouts: 292 us -> 11.7 us
  Pallas kernels: 0 us -> 57.8 us
  blocking collectives: 47.1 us -> 0 us
  other arithmetic: 18 us -> 0 us
  waiting for transfers between devices: 12.1 us -> 0 us
    dot_general x26 -> x0, matrix products: 796 us -> none  [the longest x11 390 us: grid_block(): jnp.einsum('km,mv->vk', imag_basis, imag_cols, preferred_element_type=jnp...]
    another operation x4 -> x0, local copies, waits for them, and re-layouts: 183 us -> none  [the longest x1 183 us: shards(): columns = own_rows[:, :, 0, :].reshape(TRUNC, levels, 2)]
    slice x1 -> x0, local copies, waits for them, and re-layouts: 83.6 us -> none  [shards(): imag_cols = columns[:, :, 1]]
    pallas_call x0 -> x2, Pallas kernels: none -> 57.8 us  [the longest x1 46.6 us: shards(): pl.pallas_call(exchange_kernel, grid=(STEPS,), out_shape=[jax.ShapeDtypeS...]
    all_to_all x1 -> x0, blocking collectives: 47.1 us -> none  [shards(): lax.all_to_all(ordered, 'wave', split_axis=2, concat_axis=0, tiled=True)]
    all_to_all x1 -> x0, waiting for transfers between devices: 12.1 us -> none  [shards(): lax.all_to_all(partial_rows, 'lev', split_axis=2, concat_axis=3, tiled=True)]
  transfers between devices with their start and end apart: 1 -> 0, of which waited for: 1 -> 0; matrix products, arithmetic and copies ran while one was open for 0% -> 0% of each run, Pallas kernels for 0% -> 0%
where the time goes in v1:
time: 69.8 us; the launch traced here: 69.5 us
  Pallas kernels  57.8 us (83%)
  local copies, waits for them, and re-layouts  11.7 us (17%)
    pallas_call x1, Pallas kernels, shards(): pl.pallas_call(exchange_kernel, grid=(STEPS,), out_shape=[jax.ShapeDtypeS...  46.6 us
    pallas_call x1, Pallas kernels, shards(): pl.pallas_call(fourier_kernel, grid=(BLOCKS,), out_shape=jax.ShapeDtypeSt...  11.2 us
    unnamed x18, local copies, waits for them, and re-layouts  11 us

profile of v1, /device:TPU:1, one launch (start us, length us, event | category | flops | bytes accessed | tf_op | source)
XLA Modules:
  0.0 69.5 jit_solution(12127432425272393637)
XLA Ops:
  0.0 0.7 reshape.6.pair_v
  0.7 0.0 copy-start
  0.7 1.4 %copy-done = bf16[10,641,128]{2,1,0:T(8,128)(2,1)S(1)} copy-done((bf16[10,641,128]{2,1,0:T(8,128)(2,1)S(1)}, bf16[10,641,128]{2,1,0:T(8,128)(2,1)}, u32[]{:S(2)}) %copy-start) | copy-done | bytes 1640984
  2.1 0.0 copy-start.1
  2.1 1.4 %copy-done.1 = bf16[10,641,128]{2,1,0:T(8,128)(2,1)S(1)} copy-done((bf16[10,641,128]{2,1,0:T(8,128)(2,1)S(1)}, bf16[10,641,128]{2,1,0:T(8,128)(2,1)}, u32[]{:S(2)}) %copy-start.1) | copy-done | bytes 1640984
  3.6 0.0 copy-start.2
  3.6 1.4 %copy-done.2 = bf16[10,640,128]{2,1,0:T(8,128)(2,1)S(1)} copy-done((bf16[10,640,128]{2,1,0:T(8,128)(2,1)S(1)}, bf16[10,640,128]{2,1,0:T(8,128)(2,1)}, u32[]{:S(2)}) %copy-start.2) | copy-done | bytes 1638424
  5.0 0.0 copy-start.3
  5.0 1.4 %copy-done.3 = bf16[10,640,128]{2,1,0:T(8,128)(2,1)S(1)} copy-done((bf16[10,640,128]{2,1,0:T(8,128)(2,1)S(1)}, bf16[10,640,128]{2,1,0:T(8,128)(2,1)}, u32[]{:S(2)}) %copy-start.3) | copy-done | bytes 1638424
  6.4 0.0 copy-start.4
  6.4 0.7 copy-done.4
  7.1 0.0 copy-start.5
  7.1 0.7 copy-done.5
  7.8 0.0 copy-start.7
  7.8 0.7 copy-done.7
  8.5 0.0 copy-start.6
  8.5 46.6 %legendre_exchange.1 = (bf16[256,10,2,128]{3,2,1,0:T(2,128)(2,1)S(1)}, bf16[2,1280,1536]{2,1,0:T(8,128)(2,1)}) custom-call(s32[640]{0:T(1024)S(1)} %copy-done.4, s32[256]{0:T(256)S(1)} %copy-done.5, s32[128]{0:T(128)S(1)} %copy-done.7, s32[1,640]{1,0:T(1,128)S(1)} %reshape.6.pair_v, s32[1,256]{1,0:T(1,128)S(1)} %bitcast.1, ...), custom_call_target="tpu_custom_call" | custom-call | flops 839516160 | bytes 16777216 | tf_op jit(solution)/shard_map/legendre_exchange/pallas_call | solution.py:279
  55.0 0.0 copy-done.6
  55.0 0.0 copy-start.8
  55.1 3.2 %copy-done.8 = bf16[2,1280,1536]{2,1,0:T(8,128)(2,1)S(1)} copy-done((bf16[2,1280,1536]{2,1,0:T(8,128)(2,1)S(1)}, bf16[2,1280,1536]{2,1,0:T(8,128)(2,1)}, u32[]{:S(2)}) %copy-start.8) | copy-done | bytes 7864344
  58.3 11.2 %fourier.1 = bf16[1,256,5632]{2,1,0:T(8,128)(2,1)} custom-call(s32[256]{0:T(256)S(1)} %copy-done.6, s32[128]{0:T(128)S(1)} %copy-done.7, s32[1,640]{1,0:T(1,128)S(1)} %reshape.6.pair_v, bf16[256,10,2,128]{3,2,1,0:T(2,128)(2,1)S(1)} %get-tuple-element.7.recv, bf16[2,1280,1536]{2,1,0:T(8,128)(2,1)S(1)} %copy-done.8), custom_call_target="tpu_custom_call" | custom-call | flops 4026531840 | bytes 12582912 | tf_op jit(solution)/shard_map/fourier/pallas_call | solution.py:320
Async XLA Ops:
  0.7 1.4 %copy-start = (bf16[10,641,128]{2,1,0:T(8,128)(2,1)S(1)}, bf16[10,641,128]{2,1,0:T(8,128)(2,1)}, u32[]{:S(2)}) copy-start(bf16[10,641,128]{2,1,0:T(8,128)(2,1)} %spec_even.1) | copy-start | bytes 4922884
  2.1 1.4 %copy-start.1 = (bf16[10,641,128]{2,1,0:T(8,128)(2,1)S(1)}, bf16[10,641,128]{2,1,0:T(8,128)(2,1)}, u32[]{:S(2)}) copy-start(bf16[10,641,128]{2,1,0:T(8,128)(2,1)} %tab_even.1) | copy-start | bytes 4922884
  3.6 1.4 %copy-start.2 = (bf16[10,640,128]{2,1,0:T(8,128)(2,1)S(1)}, bf16[10,640,128]{2,1,0:T(8,128)(2,1)}, u32[]{:S(2)}) copy-start(bf16[10,640,128]{2,1,0:T(8,128)(2,1)} %spec_odd.1) | copy-start | bytes 4915204
  5.0 1.4 %copy-start.3 = (bf16[10,640,128]{2,1,0:T(8,128)(2,1)S(1)}, bf16[10,640,128]{2,1,0:T(8,128)(2,1)}, u32[]{:S(2)}) copy-start(bf16[10,640,128]{2,1,0:T(8,128)(2,1)} %tab_odd.1) | copy-start | bytes 4915204
  6.4 0.7 copy-start.4
  7.1 0.7 copy-start.5
  7.8 0.7 copy-start.7
  8.5 46.6 %copy-start.6 = (s32[256]{0:T(256)S(1)}, s32[256]{0:T(256)}, u32[]{:S(2)}) copy-start(s32[256]{0:T(256)} %row_s.3) | copy-start | bytes 3076
  55.0 3.2 %copy-start.8 = (bf16[2,1280,1536]{2,1,0:T(8,128)(2,1)S(1)}, bf16[2,1280,1536]{2,1,0:T(8,128)(2,1)}, u32[]{:S(2)}) copy-start(bf16[2,1280,1536]{2,1,0:T(8,128)(2,1)} %get-tuple-element.8.basis) | copy-start | bytes 23592964

commit v2 on v1

v2 whole, which is shorter than its diff:
```python
import math

import jax
import jax.numpy as jnp
from jax import lax
from jax.experimental import pallas as pl
from jax.experimental.pallas import tpu as pltpu
from jax.sharding import PartitionSpec as P

TRUNC = 1280
SLOTS = 640
LPAD = 5632
ROWS = 256
PAIRS = 128
WAVE = 64
LEV = 4
SLOTS_DEV = 10
MESSAGE = 2 * SLOTS_DEV
LOADS = ((0, 2), (2, 4), (6, 4))
QUARTER_PAD = 1408
LANES = 128
COLUMN_BLOCKS = ((0, 512), (512, 512), (1024, 384))
ROW_CHUNK = 128
ARRIVALS = ((0, 32, 384, 0), (32, 24, 256, 768), (56, 8, 128, 1280))
TERMS = 1536
GROUP = 16
BARRIER_LOAD = 1

MESH = pl.DeviceIdType.MESH
VMEM = pltpu.VMEM
SMEM = pltpu.SMEM
F32 = jnp.float32
BF16 = jnp.bfloat16
TN = (((0,), (0,)), ((), ()))
NT = (((1,), (1,)), ((), ()))


def lane_iota(rows):
    return lax.broadcasted_iota(jnp.int32, (rows, LANES), 1)


def unit_circle(product, length, inverse):
    rest = product - jnp.floor(product * inverse) * length
    quarters = rest * (4.0 * inverse)
    nearest = jnp.floor(quarters + 0.5)
    angle = (quarters - nearest) * (0.5 * math.pi)
    z = angle * angle
    sine = angle * (1.0 + z * (-1.0 / 6 + z * (1.0 / 120 + z * (-1.0 / 5040 + z * (1.0 / 362880)))))
    cosine = 1.0 + z * (-0.5 + z * (1.0 / 24 + z * (-1.0 / 720 + z * (1.0 / 40320))))
    quadrant = nearest.astype(jnp.int32)
    odd = (quadrant & 1) == 1
    cos_out = jnp.where(odd, sine, cosine)
    sin_out = jnp.where(odd, cosine, sine)
    cos_out = jnp.where(((quadrant + 1) & 2) == 2, -cos_out, cos_out)
    sin_out = jnp.where((quadrant & 2) == 2, -sin_out, sin_out)
    return cos_out, sin_out


def masked_halves(coeffs, count, flip):
    rows = coeffs.shape[0]
    position = lax.broadcasted_iota(jnp.int32, (rows, LANES), 0)
    first = jnp.where(position < count, 1.0, 0.0)
    chosen = (flip + (1.0 - 2.0 * flip) * first).astype(BF16)
    even = coeffs * chosen
    return jnp.concatenate([even, coeffs - even], axis=1)


def exchange_kernel(
    pair_s,
    row_s,
    length_s,
    pair_v,
    row_v,
    spec_even_in,
    spec_odd_in,
    tab_even_in,
    tab_odd_in,
    quarters_out,
    spec_even,
    spec_odd,
    tab_even,
    tab_odd,
    permute,
    spread,
    send,
    recv,
    waves,
    basis,
    left,
    total,
    quarters,
    send_sem,
    recv_sem,
    self_sem,
    load_sem,
    out_sem,
    line_sem,
):
    w = lax.axis_index("wave")
    l = lax.axis_index("lev")
    me = w * LEV + l
    barrier = pltpu.get_barrier_semaphore()

    def in_plane(i):
        return (w - lax.rem(w, GROUP) + lax.rem(w + i, GROUP), l)

    def across(i):
        return (lax.rem(w + i // LEV * GROUP, WAVE), lax.rem(l + i, LEV))

    loads = []
    for number, (begin, count) in enumerate(LOADS):
        slots = pl.ds(begin, count)
        loads.append(
            [
                pltpu.make_async_copy(source.at[slots], held.at[slots], load_sem.at[i, number])
                for i, (source, held) in enumerate(
                    (
                        (spec_even_in, spec_even),
                        (tab_even_in, tab_even),
                        (spec_odd_in, spec_odd),
                        (tab_odd_in, tab_odd),
                    )
                )
            ]
        )
    for copy in loads[0]:
        copy.start()
    for i in range(1, GROUP):
        pl.semaphore_signal(barrier, inc=1, device_id=in_plane(i), device_id_type=MESH)
        pl.semaphore_signal(barrier, inc=1, device_id=across(i), device_id_type=MESH)
    for copies in loads[1:]:
        for copy in copies:
            copy.start()
    source = lax.broadcasted_iota(jnp.int32, (ROWS, ROWS), 0)
    hot = jnp.where(source == row_v[...].reshape(1, ROWS), 1.0, 0.0)
    permute[...] = hot.T.astype(BF16)

    def one_slot(slot):
        first = pair_s[w * SLOTS_DEV + slot]
        flip = (first & 1).astype(F32)
        even_terms = masked_halves(spec_even[slot], (TRUNC + 1 - first) >> 1, flip)
        odd_terms = masked_halves(spec_odd[slot], (TRUNC - first) >> 1, flip)
        sym = lax.dot_general(tab_even[slot], even_terms, TN, preferred_element_type=F32)
        anti = lax.dot_general(tab_odd[slot], odd_terms, TN, preferred_element_type=F32)
        rows = jnp.concatenate([sym + anti, sym - anti], axis=0).astype(BF16)
        ordered = jnp.dot(permute[...], rows, preferred_element_type=F32)
        spread[pl.ds(slot, ROWS, stride=MESSAGE), :] = ordered[:, :LANES]
        spread[pl.ds(slot + SLOTS_DEV, ROWS, stride=MESSAGE), :] = ordered[:, LANES:]

    for number, (begin, count) in enumerate(LOADS):
        for copy in loads[number]:
            copy.wait()

        def two_slots(i, carry, begin=begin):
            one_slot(begin + 2 * i)
            one_slot(begin + 2 * i + 1)
            return carry

        lax.fori_loop(0, count // 2, two_slots, 0)
        if number == BARRIER_LOAD:
            pl.semaphore_wait(barrier, 2 * (GROUP - 1))
            for i in range(1, GROUP):
                pl.semaphore_signal(line_sem, inc=1, device_id=across(i), device_id_type=MESH)

    pl.semaphore_wait(line_sem, GROUP - 1)

    def pack(back):
        target = lax.rem(w - back + WAVE, WAVE)
        start = pl.multiple_of(target * (LEV * MESSAGE), LEV * MESSAGE)
        block = spread[pl.ds(start, LEV * MESSAGE), :].astype(BF16)
        send[pl.ds(target * LEV, LEV)] = block.reshape(LEV, MESSAGE // 2, 2, LANES)
        return target

    def send_one(target, back, turn, part):
        lev = lax.rem(l - turn + LEV, LEV)
        pltpu.make_async_remote_copy(
            src_ref=send.at[target * LEV + lev],
            dst_ref=recv.at[l * WAVE + back],
            send_sem=send_sem,
            recv_sem=recv_sem.at[part],
            device_id=(target, lev),
            device_id_type=MESH,
        ).start()

    target = pack(0)
    for turn in range(1, LEV):
        send_one(target, 0, turn, 0)
    own = pltpu.make_async_copy(send.at[me], recv.at[l * WAVE], self_sem)
    own.start()
    for part, (begin, count, _, _) in enumerate(ARRIVALS):

        def send_four(back, carry, part=part):
            target = pack(back)
            for turn in range(LEV):
                send_one(target, back, turn, part)
            return carry

        lax.fori_loop(max(begin, 1), begin + count, send_four, 0)

    length = length_s[row_s[me] & (PAIRS - 1)]
    quarter = length >> 2
    length = length.astype(F32)
    inverse = 1.0 / jnp.full((16, LANES), length, F32)
    pairs = pair_v[...].reshape(1, SLOTS)
    for i in range(SLOTS // LANES):
        pair = pairs[:, i * LANES : (i + 1) * LANES]
        even = jnp.where((pair & 1) == 0, pair, TRUNC - 1 - pair).astype(F32)
        column = jnp.broadcast_to(even, (LANES, LANES)).T
        for start in range(i * LANES, 2 * SLOTS + LANES, SLOTS):
            waves[start : start + LANES, :] = column

    lane = lane_iota(16).astype(F32)
    left[...] = jnp.zeros_like(left)
    for _, count, padded, offset in ARRIVALS:
        used = count * SLOTS_DEV
        blank = jnp.zeros((2, padded - used, QUARTER_PAD), BF16)
        basis[:, offset + used : offset + padded, :] = blank
        basis[:, offset + padded + used : offset + 2 * padded, :] = blank

    for begin, count, padded, offset in ARRIVALS:

        def basis_rows(i, carry, begin=begin, padded=padded, offset=offset):
            at = pl.multiple_of(offset + i * 16, 16)
            low = pl.multiple_of(offset + padded + i * 16, 16)
            even = waves[pl.ds(SLOTS_DEV * (w + begin) + i * 16, 16), :]
            for parity in range(2):
                number = even if parity == 0 else (TRUNC - 1.0) - even
                factor = jnp.where(
                    2.0 * number < length, jnp.where(number == 0.0, 1.0, 2.0), 0.0
                )
                cosine, sine = unit_circle(number * lane, length, inverse)
                turn_cos, turn_sin = unit_circle(number * float(LANES), length, inverse)
                real = factor * cosine
                imag = -factor * sine
                for k in range(QUARTER_PAD // LANES):
                    columns = slice(k * LANES, (k + 1) * LANES)
                    basis[parity, pl.ds(at, 16), columns] = real.astype(BF16)
                    basis[parity, pl.ds(low, 16), columns] = imag.astype(BF16)
                    real, imag = (
                        real * turn_cos + imag * turn_sin,
                        imag * turn_cos - real * turn_sin,
                    )
            return carry

        lax.fori_loop(0, count * SLOTS_DEV // 16, basis_rows, 0)

    row = lax.broadcasted_iota(jnp.int32, (LANES, LANES), 0)
    wanted = jnp.where(row < 64, 2 * row, 2 * row - 127)
    pick = jnp.where(lane_iota(LANES) == wanted, 1.0, 0.0).astype(BF16)
    own.wait()
    for part, (begin, count, padded, offset) in enumerate(ARRIVALS):
        used = count * SLOTS_DEV
        held = pl.ds(0, count * LEV - (1 if part == 0 else 0))
        pltpu.make_async_copy(send.at[held], recv.at[held], recv_sem.at[part]).wait()
        column = waves[pl.ds(SLOTS_DEV * (w + begin), padded), :]
        evens = column.T[:1, :used].astype(jnp.int32)
        for parity in range(2):
            number = evens if parity == 0 else TRUNC - 1 - evens
            second = ((number >> 1) & 1).astype(F32)
            sign = 1.0 - 2.0 * second if parity == 0 else 2.0 * second - 1.0
            for lev in range(LEV):
                first = lev * WAVE + begin
                block = recv[first : first + count, parity * 5 : parity * 5 + 5]
                block = block.reshape(used, LANES)
                parts = lax.dot_general(pick, block, NT, preferred_element_type=F32)
                real, imag = parts[:64], parts[64:]
                top = slice(lev * 64, lev * 64 + 64)
                low = slice(256 + lev * 64, 256 + lev * 64 + 64)
                at = slice(offset, offset + used)
                after = slice(offset + padded, offset + padded + used)
                left[parity, top, at] = real.astype(BF16)
                left[parity, top, after] = imag.astype(BF16)
                if parity == 0:
                    left[parity, low, at] = (real * sign).astype(BF16)
                    left[parity, low, after] = (imag * sign).astype(BF16)
                else:
                    left[parity, low, at] = (imag * sign).astype(BF16)
                    left[parity, low, after] = (real * -sign).astype(BF16)
        terms = slice(offset, offset + 2 * padded)
        for number, (origin, width) in enumerate(COLUMN_BLOCKS):
            columns = slice(origin, origin + width)
            sums = [
                jnp.dot(
                    left[parity, :, terms],
                    basis[parity, terms, columns],
                    preferred_element_type=F32,
                )
                for parity in range(2)
            ]
            if part > 0:
                sums = [total[parity, :, columns] + sums[parity] for parity in range(2)]
            if part < len(ARRIVALS) - 1:
                for parity in range(2):
                    total[parity, :, columns] = sums[parity]
                continue
            even, odd = sums
            point = origin + lax.broadcasted_iota(jnp.int32, (256, width), 1)
            inside = point < quarter
            for c in range(4):
                half = slice((c & 1) * 256, (c & 1) * 256 + 256)
                value = even[half] + odd[half] if c < 2 else even[half] - odd[half]
                quarters[c, :, columns] = jnp.where(inside, value, 0.0).astype(BF16)
            pltpu.make_async_copy(
                quarters.at[:, :, pl.ds(origin, width)],
                quarters_out.at[:, :, pl.ds(origin, width)],
                out_sem.at[number],
            ).start()
    others = pl.ds(0, ROWS - 1)
    pltpu.make_async_copy(send.at[others], recv.at[others], send_sem).wait()
    for number, (origin, width) in enumerate(COLUMN_BLOCKS):
        pltpu.make_async_copy(
            quarters.at[:, :, pl.ds(origin, width)],
            quarters_out.at[:, :, pl.ds(origin, width)],
            out_sem.at[number],
        ).wait()


def place_kernel(row_s, length_s, quarters, grid_out):
    me = lax.axis_index("wave") * LEV + lax.axis_index("lev")
    quarter = length_s[row_s[me] & (PAIRS - 1)] >> 2
    grid_out[...] = jnp.zeros_like(grid_out)
    lane = lane_iota(ROW_CHUNK)
    tiles = QUARTER_PAD // LANES
    for c in range(4):
        offset = c * quarter
        shift = offset & (LANES - 1)
        start = pl.multiple_of(offset - shift, LANES)
        before = lane < shift
        previous = jnp.zeros((ROW_CHUNK, LANES), F32)
        for i in range(tiles + 1):
            if i < tiles:
                tile = quarters[c, :, i * LANES : (i + 1) * LANES].astype(F32)
                turned = pltpu.roll(tile, shift, 1)
            else:
                turned = jnp.zeros((ROW_CHUNK, LANES), F32)
            piece = jnp.where(before, previous, turned).astype(BF16)
            previous = turned
            where = pl.ds(pl.multiple_of(start + i * LANES, LANES), LANES)
            if i == 0:
                grid_out[0, :, where] += piece
            else:
                grid_out[0, :, where] = piece


def shards(spectral_even, spectral_odd, table_even, table_odd, slot_pair, slot_row, row_length):
    in_smem = pl.BlockSpec(memory_space=SMEM)
    in_vmem = pl.BlockSpec(memory_space=VMEM)
    anywhere = pl.BlockSpec(memory_space=pl.ANY)
    coefficients = (spectral_even, spectral_odd, table_even, table_odd)

    message = (MESSAGE // 2, 2, LANES)
    quarters = pl.pallas_call(
        exchange_kernel,
        out_shape=jax.ShapeDtypeStruct((4, 256, QUARTER_PAD), BF16),
        in_specs=[in_smem] * 3 + [in_vmem] * 2 + [anywhere] * 4,
        out_specs=anywhere,
        scratch_shapes=[VMEM(a.shape, BF16) for a in coefficients]
        + [
            VMEM((ROWS, ROWS), BF16),
            VMEM((ROWS * MESSAGE, LANES), F32),
            VMEM((ROWS,) + message, BF16),
            VMEM((ROWS,) + message, BF16),
            VMEM((2 * SLOTS + LANES, LANES), F32),
            VMEM((2, TERMS, QUARTER_PAD), BF16),
            VMEM((2, 512, TERMS), BF16),
            VMEM((2, 512, QUARTER_PAD), F32),
            VMEM((4, 256, QUARTER_PAD), BF16),
            pltpu.SemaphoreType.DMA,
            pltpu.SemaphoreType.DMA((len(ARRIVALS),)),
            pltpu.SemaphoreType.DMA,
            pltpu.SemaphoreType.DMA((4, len(LOADS))),
            pltpu.SemaphoreType.DMA((len(COLUMN_BLOCKS),)),
            pltpu.SemaphoreType.REGULAR,
        ],
        name="legendre_exchange_fourier",
        compiler_params=pltpu.CompilerParams(
            collective_id=0, has_side_effects=True, vmem_limit_bytes=60 << 20
        ),
        cost_estimate=pl.CostEstimate(
            flops=4 * 512 * TERMS * QUARTER_PAD, bytes_accessed=10 << 20, transcendentals=0
        ),
    )(
        slot_pair,
        slot_row,
        row_length,
        slot_pair,
        slot_row,
        *coefficients,
    )
    return pl.pallas_call(
        place_kernel,
        grid=(256 // ROW_CHUNK,),
        out_shape=jax.ShapeDtypeStruct((1, 256, LPAD), BF16),
        in_specs=[
            in_smem,
            in_smem,
            pl.BlockSpec((4, ROW_CHUNK, QUARTER_PAD), lambda i: (0, i, 0)),
        ],
        out_specs=pl.BlockSpec((1, ROW_CHUNK, LPAD), lambda i: (0, i, 0)),
        name="place",
        compiler_params=pltpu.CompilerParams(vmem_limit_bytes=60 << 20),
        cost_estimate=pl.CostEstimate(flops=1 << 22, bytes_accessed=6 << 20, transcendentals=0),
    )(slot_row, row_length, quarters)


def solution(mesh):
    in_specs = (
        P("wave", None, "lev"),
        P("wave", None, "lev"),
        P("wave", None, None),
        P("wave", None, None),
        P(),
        P(),
        P(),
    )
    out_specs = P(("wave", "lev"), None, None)
    return jax.shard_map(shards, mesh=mesh, in_specs=in_specs, out_specs=out_specs, check_vma=False)
```

time: 69.8 us -> 54.2 us (0.78)
  local copies, waits for them, and re-layouts: 11.7 us -> 0 us
  Pallas kernels: 57.8 us -> 53.6 us
    unnamed x18 -> x0, local copies, waits for them, and re-layouts: 11 us -> none
    pallas_call x2, Pallas kernels: 57.8 us -> 53.6 us  [the longest x1 50.1 us: shards(): pl.pallas_call(exchange_kernel, out_shape=jax.ShapeDtypeStruct((4, 256, Q...]
where the time goes in v2:
time: 54.2 us; the launch traced here: 53.6 us
  Pallas kernels  53.6 us (99%)
    pallas_call x1, Pallas kernels, shards(): pl.pallas_call(exchange_kernel, out_shape=jax.ShapeDtypeStruct((4, 256, Q...  50.1 us
    pallas_call x1, Pallas kernels, shards(): pl.pallas_call(place_kernel, grid=(256 // ROW_CHUNK,), out_shape=jax.Shap...  3.52 us

profile of v2, /device:TPU:1, one launch (start us, length us, event | category | flops | bytes accessed | tf_op | source)
XLA Modules:
  0.0 53.6 jit_solution(2426394372801914792)
XLA Ops:
  0.0 50.1 %legendre_exchange_fourier.1.quarters = bf16[4,256,1408]{2,1,0:T(8,128)(2,1)} custom-call(s32[640]{0:T(1024)} %pair_v.1, s32[256]{0:T(256)} %row_s.3, s32[128]{0:T(128)} %length_s.3, s32[640]{0:T(1024)} %pair_v.1, s32[256]{0:T(256)} %row_s.3, bf16[10,641,128]{2,1,0:T(8,128)(2,1)} %spec_even_in.1, bf16[10,640,128]{2,1,0:T(8,128)(2,1)} %spec_odd_in.1, ...), custom_call_target="tpu_custom_call" | custom-call | flops 4429185024 | bytes 10485760 | tf_op jit(solution)/shard_map/legendre_exchange_fourier/pallas_call | solution.py:352
  50.1 3.5 %place.1 = bf16[1,256,5632]{2,1,0:T(8,128)(2,1)} custom-call(s32[256]{0:T(256)} %row_s.3, s32[128]{0:T(128)} %length_s.3, bf16[4,256,1408]{2,1,0:T(8,128)(2,1)} %legendre_exchange_fourier.1.quarters), custom_call_target="tpu_custom_call" | custom-call | flops 4194304 | bytes 6291456 | tf_op jit(solution)/shard_map/place/pallas_call | solution.py:390

commit v3 on v2

--- a/solution.py
+++ b/solution.py
@@ -19,9 +19,9 @@
 LOADS = ((0, 2), (2, 4), (6, 4))
 QUARTER_PAD = 1408
 LANES = 128
-COLUMN_BLOCKS = ((0, 512), (512, 512), (1024, 384))
+COLUMN_BLOCKS = ((0, 512), (512, 512), (1024, 256), (1280, 128))
 ROW_CHUNK = 128
-ARRIVALS = ((0, 32, 384, 0), (32, 24, 256, 768), (56, 8, 128, 1280))
+ARRIVALS = ((0, 36, 384, 0), (36, 16, 256, 768), (52, 12, 128, 1280))
 TERMS = 1536
 GROUP = 16
 BARRIER_LOAD = 1
@@ -210,24 +210,26 @@
             waves[start : start + LANES, :] = column
 
     lane = lane_iota(16).astype(F32)
+    row_number = lax.broadcasted_iota(jnp.int32, (16, LANES), 0)
     left[...] = jnp.zeros_like(left)
     for _, count, padded, offset in ARRIVALS:
-        used = count * SLOTS_DEV
-        blank = jnp.zeros((2, padded - used, QUARTER_PAD), BF16)
-        basis[:, offset + used : offset + padded, :] = blank
-        basis[:, offset + padded + used : offset + 2 * padded, :] = blank
+        made = -(-count * SLOTS_DEV // 16) * 16
+        if made < padded:
+            blank = jnp.zeros((2, padded - made, QUARTER_PAD), BF16)
+            basis[:, offset + made : offset + padded, :] = blank
+            basis[:, offset + padded + made : offset + 2 * padded, :] = blank
 
     for begin, count, padded, offset in ARRIVALS:
 
-        def basis_rows(i, carry, begin=begin, padded=padded, offset=offset):
+        def basis_rows(i, carry, begin=begin, count=count, padded=padded, offset=offset):
+            real_row = i * 16 + row_number < count * SLOTS_DEV
             at = pl.multiple_of(offset + i * 16, 16)
             low = pl.multiple_of(offset + padded + i * 16, 16)
             even = waves[pl.ds(SLOTS_DEV * (w + begin) + i * 16, 16), :]
             for parity in range(2):
                 number = even if parity == 0 else (TRUNC - 1.0) - even
-                factor = jnp.where(
-                    2.0 * number < length, jnp.where(number == 0.0, 1.0, 2.0), 0.0
-                )
+                active = (2.0 * number < length) & real_row
+                factor = jnp.where(active, jnp.where(number == 0.0, 1.0, 2.0), 0.0)
                 cosine, sine = unit_circle(number * lane, length, inverse)
                 turn_cos, turn_sin = unit_circle(number * float(LANES), length, inverse)
                 real = factor * cosine
@@ -242,7 +244,7 @@
                     )
             return carry
 
-        lax.fori_loop(0, count * SLOTS_DEV // 16, basis_rows, 0)
+        lax.fori_loop(0, -(-count * SLOTS_DEV // 16), basis_rows, 0)
 
     row = lax.broadcasted_iota(jnp.int32, (LANES, LANES), 0)
     wanted = jnp.where(row < 64, 2 * row, 2 * row - 127)
@@ -326,14 +328,14 @@
         shift = offset & (LANES - 1)
         start = pl.multiple_of(offset - shift, LANES)
         before = lane < shift
-        previous = jnp.zeros((ROW_CHUNK, LANES), F32)
+        previous = jnp.zeros((ROW_CHUNK, LANES), BF16)
         for i in range(tiles + 1):
             if i < tiles:
-                tile = quarters[c, :, i * LANES : (i + 1) * LANES].astype(F32)
+                tile = quarters[c, :, i * LANES : (i + 1) * LANES]
                 turned = pltpu.roll(tile, shift, 1)
             else:
-                turned = jnp.zeros((ROW_CHUNK, LANES), F32)
-            piece = jnp.where(before, previous, turned).astype(BF16)
+                turned = jnp.zeros((ROW_CHUNK, LANES), BF16)
+            piece = jnp.where(before, previous, turned)
             previous = turned
             where = pl.ds(pl.multiple_of(start + i * LANES, LANES), LANES)
             if i == 0:

time: 54.2 us -> 53.7 us (level)
  no operation moved by 1% of the time
where the time goes in v3:
time: 53.7 us; the launch traced here: 53.6 us
  Pallas kernels  53.6 us (100%)
    pallas_call x1, Pallas kernels, shards(): pl.pallas_call(exchange_kernel, out_shape=jax.ShapeDtypeStruct((4, 256, Q...  50.2 us
    pallas_call x1, Pallas kernels, shards(): pl.pallas_call(place_kernel, grid=(256 // ROW_CHUNK,), out_shape=jax.Shap...  3.41 us

profile of v3, /device:TPU:1, one launch (start us, length us, event | category | flops | bytes accessed | tf_op | source)
XLA Modules:
  0.0 53.6 jit_solution(16799264704343706229)
XLA Ops:
  0.0 50.2 %legendre_exchange_fourier.1.quarters = bf16[4,256,1408]{2,1,0:T(8,128)(2,1)} custom-call(s32[640]{0:T(1024)} %pair_v.1, s32[256]{0:T(256)} %row_s.3, s32[128]{0:T(128)} %length_s.3, s32[640]{0:T(1024)} %pair_v.1, s32[256]{0:T(256)} %row_s.3, bf16[10,641,128]{2,1,0:T(8,128)(2,1)} %spec_even_in.1, bf16[10,640,128]{2,1,0:T(8,128)(2,1)} %spec_odd_in.1, ...), custom_call_target="tpu_custom_call" | custom-call | flops 4429185024 | bytes 10485760 | tf_op jit(solution)/shard_map/legendre_exchange_fourier/pallas_call | solution.py:354
  50.2 3.4 %place.1 = bf16[1,256,5632]{2,1,0:T(8,128)(2,1)} custom-call(s32[256]{0:T(256)} %row_s.3, s32[128]{0:T(128)} %length_s.3, bf16[4,256,1408]{2,1,0:T(8,128)(2,1)} %legendre_exchange_fourier.1.quarters), custom_call_target="tpu_custom_call" | custom-call | flops 4194304 | bytes 6291456 | tf_op jit(solution)/shard_map/place/pallas_call | solution.py:392

commit v4 on v1

v4 whole, which is shorter than its diff:
```python
import math

import jax
import jax.numpy as jnp
from jax import lax
from jax.experimental import pallas as pl
from jax.experimental.pallas import tpu as pltpu
from jax.sharding import PartitionSpec as P

TRUNC = 1280
SLOTS = 640
LPAD = 5632
ROWS = 256
PAIRS = 128
WAVE = 64
LEV = 4
SLOTS_DEV = 10
MESSAGE = 2 * SLOTS_DEV
STEP_SLOTS = 2
STEPS = SLOTS_DEV // STEP_SLOTS
QUARTER_PAD = 1408
LANES = 128
COLUMN_BLOCKS = ((0, 512), (512, 512), (1024, 256), (1280, 128))
ROW_CHUNK = 128
ARRIVALS = ((0, 36, 384, 0), (36, 16, 256, 768), (52, 12, 128, 1280))
TERMS = 1536
GROUP = 16
BARRIER_STEP = 3

MESH = pl.DeviceIdType.MESH
VMEM = pltpu.VMEM
SMEM = pltpu.SMEM
F32 = jnp.float32
BF16 = jnp.bfloat16
TN = (((0,), (0,)), ((), ()))
NT = (((1,), (1,)), ((), ()))


def lane_iota(rows):
    return lax.broadcasted_iota(jnp.int32, (rows, LANES), 1)


def unit_circle(product, length, inverse):
    rest = product - jnp.floor(product * inverse) * length
    quarters = rest * (4.0 * inverse)
    nearest = jnp.floor(quarters + 0.5)
    angle = (quarters - nearest) * (0.5 * math.pi)
    z = angle * angle
    sine = angle * (1.0 + z * (-1.0 / 6 + z * (1.0 / 120 + z * (-1.0 / 5040 + z * (1.0 / 362880)))))
    cosine = 1.0 + z * (-0.5 + z * (1.0 / 24 + z * (-1.0 / 720 + z * (1.0 / 40320))))
    quadrant = nearest.astype(jnp.int32)
    odd = (quadrant & 1) == 1
    cos_out = jnp.where(odd, sine, cosine)
    sin_out = jnp.where(odd, cosine, sine)
    cos_out = jnp.where(((quadrant + 1) & 2) == 2, -cos_out, cos_out)
    sin_out = jnp.where((quadrant & 2) == 2, -sin_out, sin_out)
    return cos_out, sin_out


def masked_halves(coeffs, count, flip):
    rows = coeffs.shape[0]
    position = lax.broadcasted_iota(jnp.int32, (rows, LANES), 0)
    first = jnp.where(position < count, 1.0, 0.0)
    chosen = (flip + (1.0 - 2.0 * flip) * first).astype(BF16)
    even = coeffs * chosen
    return jnp.concatenate([even, coeffs - even], axis=1)


def exchange_kernel(
    pair_s,
    row_s,
    length_s,
    pair_v,
    row_v,
    spec_even,
    spec_odd,
    tab_even,
    tab_odd,
    quarters_out,
    permute,
    spread,
    send,
    recv,
    waves,
    basis,
    left,
    total,
    quarters,
    send_sem,
    recv_sem,
    self_sem,
    out_sem,
    line_sem,
):
    step = pl.program_id(0)
    w = lax.axis_index("wave")
    l = lax.axis_index("lev")
    me = w * LEV + l
    barrier = pltpu.get_barrier_semaphore()

    def in_plane(i):
        return (w - lax.rem(w, GROUP) + lax.rem(w + i, GROUP), l)

    def across(i):
        return (lax.rem(w + i // LEV * GROUP, WAVE), lax.rem(l + i, LEV))

    @pl.when(step == 0)
    def _():
        for i in range(1, GROUP):
            pl.semaphore_signal(barrier, inc=1, device_id=in_plane(i), device_id_type=MESH)
            pl.semaphore_signal(barrier, inc=1, device_id=across(i), device_id_type=MESH)
        source = lax.broadcasted_iota(jnp.int32, (ROWS, ROWS), 0)
        hot = jnp.where(source == row_v[...].reshape(1, ROWS), 1.0, 0.0)
        permute[...] = hot.T.astype(BF16)

    @pl.when(step == BARRIER_STEP)
    def _():
        pl.semaphore_wait(barrier, 2 * (GROUP - 1))
        for i in range(1, GROUP):
            pl.semaphore_signal(line_sem, inc=1, device_id=across(i), device_id_type=MESH)

    for j in range(STEP_SLOTS):
        slot = step * STEP_SLOTS + j
        first = pair_s[w * SLOTS_DEV + slot]
        flip = (first & 1).astype(F32)
        even_terms = masked_halves(spec_even[j], (TRUNC + 1 - first) >> 1, flip)
        odd_terms = masked_halves(spec_odd[j], (TRUNC - first) >> 1, flip)
        sym = lax.dot_general(tab_even[j], even_terms, TN, preferred_element_type=F32)
        anti = lax.dot_general(tab_odd[j], odd_terms, TN, preferred_element_type=F32)
        rows = jnp.concatenate([sym + anti, sym - anti], axis=0).astype(BF16)
        ordered = jnp.dot(permute[...], rows, preferred_element_type=F32)
        spread[pl.ds(slot, ROWS, stride=MESSAGE), :] = ordered[:, :LANES]
        spread[pl.ds(slot + SLOTS_DEV, ROWS, stride=MESSAGE), :] = ordered[:, LANES:]

    @pl.when(step == STEPS - 1)
    def _():
        pl.semaphore_wait(line_sem, GROUP - 1)

        def pack(back):
            target = lax.rem(w - back + WAVE, WAVE)
            start = pl.multiple_of(target * (LEV * MESSAGE), LEV * MESSAGE)
            block = spread[pl.ds(start, LEV * MESSAGE), :].astype(BF16)
            send[pl.ds(target * LEV, LEV)] = block.reshape(LEV, MESSAGE // 2, 2, LANES)
            return target

        def send_one(target, back, turn, part):
            lev = lax.rem(l - turn + LEV, LEV)
            pltpu.make_async_remote_copy(
                src_ref=send.at[target * LEV + lev],
                dst_ref=recv.at[l * WAVE + back],
                send_sem=send_sem,
                recv_sem=recv_sem.at[part],
                device_id=(target, lev),
                device_id_type=MESH,
            ).start()

        target = pack(0)
        for turn in range(1, LEV):
            send_one(target, 0, turn, 0)
        own = pltpu.make_async_copy(send.at[me], recv.at[l * WAVE], self_sem)
        own.start()
        for part, (begin, count, _, _) in enumerate(ARRIVALS):

            def send_four(back, carry, part=part):
                target = pack(back)
                for turn in range(LEV):
                    send_one(target, back, turn, part)
                return carry

            lax.fori_loop(max(begin, 1), begin + count, send_four, 0)

        length = length_s[row_s[me] & (PAIRS - 1)]
        quarter = length >> 2
        length = length.astype(F32)
        inverse = 1.0 / jnp.full((16, LANES), length, F32)
        pairs = pair_v[...].reshape(1, SLOTS)
        for i in range(SLOTS // LANES):
            pair = pairs[:, i * LANES : (i + 1) * LANES]
            even = jnp.where((pair & 1) == 0, pair, TRUNC - 1 - pair).astype(F32)
            column = jnp.broadcast_to(even, (LANES, LANES)).T
            for start in range(i * LANES, 2 * SLOTS + LANES, SLOTS):
                waves[start : start + LANES, :] = column

        lane = lane_iota(16).astype(F32)
        row_number = lax.broadcasted_iota(jnp.int32, (16, LANES), 0)
        left[...] = jnp.zeros_like(left)
        for _, count, padded, offset in ARRIVALS:
            made = -(-count * SLOTS_DEV // 16) * 16
            if made < padded:
                blank = jnp.zeros((2, padded - made, QUARTER_PAD), BF16)
                basis[:, offset + made : offset + padded, :] = blank
                basis[:, offset + padded + made : offset + 2 * padded, :] = blank

        for begin, count, padded, offset in ARRIVALS:

            def basis_rows(i, carry, begin=begin, count=count, padded=padded, offset=offset):
                real_row = i * 16 + row_number < count * SLOTS_DEV
                at = pl.multiple_of(offset + i * 16, 16)
                low = pl.multiple_of(offset + padded + i * 16, 16)
                even = waves[pl.ds(SLOTS_DEV * (w + begin) + i * 16, 16), :]
                for parity in range(2):
                    number = even if parity == 0 else (TRUNC - 1.0) - even
                    active = (2.0 * number < length) & real_row
                    factor = jnp.where(active, jnp.where(number == 0.0, 1.0, 2.0), 0.0)
                    cosine, sine = unit_circle(number * lane, length, inverse)
                    turn_cos, turn_sin = unit_circle(number * float(LANES), length, inverse)
                    real = factor * cosine
                    imag = -factor * sine
                    for k in range(QUARTER_PAD // LANES):
                        columns = slice(k * LANES, (k + 1) * LANES)
                        basis[parity, pl.ds(at, 16), columns] = real.astype(BF16)
                        basis[parity, pl.ds(low, 16), columns] = imag.astype(BF16)
                        real, imag = (
                            real * turn_cos + imag * turn_sin,
                            imag * turn_cos - real * turn_sin,
                        )
                return carry

            lax.fori_loop(0, -(-count * SLOTS_DEV // 16), basis_rows, 0)

        row = lax.broadcasted_iota(jnp.int32, (LANES, LANES), 0)
        wanted = jnp.where(row < 64, 2 * row, 2 * row - 127)
        pick = jnp.where(lane_iota(LANES) == wanted, 1.0, 0.0).astype(BF16)
        own.wait()
        for part, (begin, count, padded, offset) in enumerate(ARRIVALS):
            used = count * SLOTS_DEV
            held = pl.ds(0, count * LEV - (1 if part == 0 else 0))
            pltpu.make_async_copy(send.at[held], recv.at[held], recv_sem.at[part]).wait()
            column = waves[pl.ds(SLOTS_DEV * (w + begin), padded), :]
            evens = column.T[:1, :used].astype(jnp.int32)
            for parity in range(2):
                number = evens if parity == 0 else TRUNC - 1 - evens
                second = ((number >> 1) & 1).astype(F32)
                sign = 1.0 - 2.0 * second if parity == 0 else 2.0 * second - 1.0
                for lev in range(LEV):
                    first = lev * WAVE + begin
                    block = recv[first : first + count, parity * 5 : parity * 5 + 5]
                    block = block.reshape(used, LANES)
                    parts = lax.dot_general(pick, block, NT, preferred_element_type=F32)
                    real, imag = parts[:64], parts[64:]
                    top = slice(lev * 64, lev * 64 + 64)
                    low = slice(256 + lev * 64, 256 + lev * 64 + 64)
                    at = slice(offset, offset + used)
                    after = slice(offset + padded, offset + padded + used)
                    left[parity, top, at] = real.astype(BF16)
                    left[parity, top, after] = imag.astype(BF16)
                    if parity == 0:
                        left[parity, low, at] = (real * sign).astype(BF16)
                        left[parity, low, after] = (imag * sign).astype(BF16)
                    else:
                        left[parity, low, at] = (imag * sign).astype(BF16)
                        left[parity, low, after] = (real * -sign).astype(BF16)
            terms = slice(offset, offset + 2 * padded)
            for number, (origin, width) in enumerate(COLUMN_BLOCKS):
                columns = slice(origin, origin + width)
                sums = [
                    jnp.dot(
                        left[parity, :, terms],
                        basis[parity, terms, columns],
                        preferred_element_type=F32,
                    )
                    for parity in range(2)
                ]
                if part > 0:
                    sums = [total[parity, :, columns] + sums[parity] for parity in range(2)]
                if part < len(ARRIVALS) - 1:
                    for parity in range(2):
                        total[parity, :, columns] = sums[parity]
                    continue
                even, odd = sums
                point = origin + lax.broadcasted_iota(jnp.int32, (256, width), 1)
                inside = point < quarter
                for c in range(4):
                    half = slice((c & 1) * 256, (c & 1) * 256 + 256)
                    value = even[half] + odd[half] if c < 2 else even[half] - odd[half]
                    quarters[c, :, columns] = jnp.where(inside, value, 0.0).astype(BF16)
                pltpu.make_async_copy(
                    quarters.at[:, :, pl.ds(origin, width)],
                    quarters_out.at[:, :, pl.ds(origin, width)],
                    out_sem.at[number],
                ).start()
        others = pl.ds(0, ROWS - 1)
        pltpu.make_async_copy(send.at[others], recv.at[others], send_sem).wait()
        for number, (origin, width) in enumerate(COLUMN_BLOCKS):
            pltpu.make_async_copy(
                quarters.at[:, :, pl.ds(origin, width)],
                quarters_out.at[:, :, pl.ds(origin, width)],
                out_sem.at[number],
            ).wait()


def place_kernel(row_s, length_s, quarters, grid_out):
    me = lax.axis_index("wave") * LEV + lax.axis_index("lev")
    quarter = length_s[row_s[me] & (PAIRS - 1)] >> 2
    grid_out[...] = jnp.zeros_like(grid_out)
    lane = lane_iota(ROW_CHUNK)
    tiles = QUARTER_PAD // LANES
    for c in range(4):
        offset = c * quarter
        shift = offset & (LANES - 1)
        start = pl.multiple_of(offset - shift, LANES)
        before = lane < shift
        previous = jnp.zeros((ROW_CHUNK, LANES), BF16)
        for i in range(tiles + 1):
            if i < tiles:
                tile = quarters[c, :, i * LANES : (i + 1) * LANES]
                turned = pltpu.roll(tile, shift, 1)
            else:
                turned = jnp.zeros((ROW_CHUNK, LANES), BF16)
            piece = jnp.where(before, previous, turned)
            previous = turned
            where = pl.ds(pl.multiple_of(start + i * LANES, LANES), LANES)
            if i == 0:
                grid_out[0, :, where] += piece
            else:
                grid_out[0, :, where] = piece


def shards(spectral_even, spectral_odd, table_even, table_odd, slot_pair, slot_row, row_length):
    in_smem = pl.BlockSpec(memory_space=SMEM)
    in_vmem = pl.BlockSpec(memory_space=VMEM)
    anywhere = pl.BlockSpec(memory_space=pl.ANY)

    def by_slot(array):
        return pl.BlockSpec((STEP_SLOTS,) + array.shape[1:], lambda i: (i, 0, 0))

    message = (MESSAGE // 2, 2, LANES)
    quarters = pl.pallas_call(
        exchange_kernel,
        grid=(STEPS,),
        out_shape=jax.ShapeDtypeStruct((4, 256, QUARTER_PAD), BF16),
        in_specs=[in_smem] * 3
        + [in_vmem] * 2
        + [by_slot(a) for a in (spectral_even, spectral_odd, table_even, table_odd)],
        out_specs=anywhere,
        scratch_shapes=[
            VMEM((ROWS, ROWS), BF16),
            VMEM((ROWS * MESSAGE + MESSAGE, LANES), F32),
            VMEM((ROWS,) + message, BF16),
            VMEM((ROWS,) + message, BF16),
            VMEM((2 * SLOTS + LANES, LANES), F32),
            VMEM((2, TERMS, QUARTER_PAD), BF16),
            VMEM((2, 512, TERMS), BF16),
            VMEM((2, 512, QUARTER_PAD), F32),
            VMEM((4, 256, QUARTER_PAD), BF16),
            pltpu.SemaphoreType.DMA,
            pltpu.SemaphoreType.DMA((len(ARRIVALS),)),
            pltpu.SemaphoreType.DMA,
            pltpu.SemaphoreType.DMA((len(COLUMN_BLOCKS),)),
            pltpu.SemaphoreType.REGULAR,
        ],
        name="legendre_exchange_fourier",
        compiler_params=pltpu.CompilerParams(
            collective_id=0, has_side_effects=True, vmem_limit_bytes=60 << 20
        ),
        cost_estimate=pl.CostEstimate(
            flops=4 * 512 * TERMS * QUARTER_PAD, bytes_accessed=10 << 20, transcendentals=0
        ),
    )(
        slot_pair,
        slot_row,
        row_length,
        slot_pair,
        slot_row,
        spectral_even,
        spectral_odd,
        table_even,
        table_odd,
    )
    return pl.pallas_call(
        place_kernel,
        grid=(256 // ROW_CHUNK,),
        out_shape=jax.ShapeDtypeStruct((1, 256, LPAD), BF16),
        in_specs=[
            in_smem,
            in_smem,
            pl.BlockSpec((4, ROW_CHUNK, QUARTER_PAD), lambda i: (0, i, 0)),
        ],
        out_specs=pl.BlockSpec((1, ROW_CHUNK, LPAD), lambda i: (0, i, 0)),
        name="place",
        compiler_params=pltpu.CompilerParams(vmem_limit_bytes=60 << 20),
        cost_estimate=pl.CostEstimate(flops=1 << 22, bytes_accessed=6 << 20, transcendentals=0),
    )(slot_row, row_length, quarters)


def solution(mesh):
    in_specs = (
        P("wave", None, "lev"),
        P("wave", None, "lev"),
        P("wave", None, None),
        P("wave", None, None),
        P(),
        P(),
        P(),
    )
    out_specs = P(("wave", "lev"), None, None)
    return jax.shard_map(shards, mesh=mesh, in_specs=in_specs, out_specs=out_specs, check_vma=False)
```

time: 69.8 us -> 54.1 us (0.78)
  local copies, waits for them, and re-layouts: 11.7 us -> 0 us
  Pallas kernels: 57.8 us -> 53.9 us
    unnamed x18 -> x0, local copies, waits for them, and re-layouts: 11 us -> none
    pallas_call x2, Pallas kernels: 57.8 us -> 53.9 us  [the longest x1 50.5 us: shards(): pl.pallas_call(exchange_kernel, grid=(STEPS,), out_shape=jax.ShapeDtypeSt...]
where the time goes in v4:
time: 54.1 us; the launch traced here: 53.9 us
  Pallas kernels  53.9 us (100%)
    pallas_call x1, Pallas kernels, shards(): pl.pallas_call(exchange_kernel, grid=(STEPS,), out_shape=jax.ShapeDtypeSt...  50.5 us
    pallas_call x1, Pallas kernels, shards(): pl.pallas_call(place_kernel, grid=(256 // ROW_CHUNK,), out_shape=jax.Shap...  3.41 us

profile of v4, /device:TPU:1, one launch (start us, length us, event | category | flops | bytes accessed | tf_op | source)
XLA Modules:
  0.0 53.9 jit_solution(11118394375566620400)
XLA Ops:
  0.0 50.5 %legendre_exchange_fourier.1.quarters = bf16[4,256,1408]{2,1,0:T(8,128)(2,1)} custom-call(s32[640]{0:T(1024)} %pair_v.1, s32[256]{0:T(256)} %row_s.3, s32[128]{0:T(128)} %length_s.3, s32[640]{0:T(1024)} %pair_v.1, s32[256]{0:T(256)} %row_s.3, bf16[10,641,128]{2,1,0:T(8,128)(2,1)} %spec_even.1, bf16[10,640,128]{2,1,0:T(8,128)(2,1)} %spec_odd.1, ...), custom_call_target="tpu_custom_call" | custom-call | flops 4429185024 | bytes 10485760 | tf_op jit(solution)/shard_map/legendre_exchange_fourier/pallas_call | solution.py:328
  50.5 3.4 %place.1 = bf16[1,256,5632]{2,1,0:T(8,128)(2,1)} custom-call(s32[256]{0:T(256)} %row_s.3, s32[128]{0:T(128)} %length_s.3, bf16[4,256,1408]{2,1,0:T(8,128)(2,1)} %legendre_exchange_fourier.1.quarters), custom_call_target="tpu_custom_call" | custom-call | flops 4194304 | bytes 6291456 | tf_op jit(solution)/shard_map/place/pallas_call | solution.py:370
